TPU v7x, 32 devices: a whole 2x2x4 slice. The times are simulated.
32 devices in a mesh: space: 8 (over z, y), sub: 4 (over x, core).
Axes of the slice: x: 2, y: 2, z: 4, core: 2. Of those that a mesh axis runs over, the one named last changes fastest.
Arguments:
- rhs: bfloat16 [4096, 1024], P(('space', 'sub')), may hold values from -6 to 6
- blocks: bfloat16 [4096, 7, 4096], P(('space', 'sub')), may hold values from -0.125 to 0.125
- columns: int32 [4096, 7], P(('space', 'sub')), may hold values from 0 to 639, as said below
- ghost_lists: int32 [32, 128], P(('space', 'sub')), may hold values from 0 to 127, as said below
Outputs:
- solution: float32 [4096, 1024], P(('space', 'sub'))
- residual: float32 [4096, 1024], P(('space', 'sub'))
Inputs may be any that keep to these rules, and one draw needn't show every extreme that they name: `columns`: for block row r (local) of device (p, q): entry 0 is q * 128 + r; entries 1 and 2 are q2 * 128 + ghost_lists[p * 4 + q2, k] for some q2 < 4 and k < 64; entries 3 and 4 lie in the part received from the previous subdomain, entries 5 and 6 in that from the next. `ghost_lists`: each row is a permutation of 0 .. 127.
All inputs are finite; a program needn't handle non-finite values.
Results may differ from a plain program's by a relative error of at most 0.0055.
Values may be sent and summed in bfloat16 or wider, within the bound.
A program may use at most 128 MiB of HBM per device.

v0:
```python
import jax
import jax.numpy as jnp
from jax import lax
from jax.sharding import PartitionSpec as P

BS = 64
NRHS = 16
NNZ = 7
S = 4


def shifted(value, axis, steps):
    count = lax.axis_size(axis)
    initial, last = (max(0, -steps), min(count, count - steps))
    return lax.ppermute(value, axis, [(source, source + steps) for source in range(initial, last)])


def finish(rhs, stack, gram):
    rows = stack.shape[0]
    paired = gram[1:] + gram[:-1]
    hmat = (paired[:, :, 1:] + paired[:, :, :-1]).reshape(S * NRHS, S * NRHS)
    cvec = paired[:, :, 0].reshape(S * NRHS, NRHS)
    lower = jnp.linalg.cholesky(hmat)
    coef = jax.scipy.linalg.cho_solve((lower, True), cvec).reshape(S, NRHS, NRHS)
    kfull = stack.astype(jnp.float32)
    highest = lax.Precision.HIGHEST
    sol = jnp.einsum("rjia,jac->ric", kfull[:, :S], coef, precision=highest)
    wmat = kfull[:, 1:] + kfull[:, :S]
    image = jnp.einsum("rjia,jac->ric", wmat, coef, precision=highest)
    res = rhs.astype(jnp.float32).reshape(rows, BS, NRHS) - image
    return (sol.reshape(rows, BS * NRHS), res.reshape(rows, BS * NRHS))


def on_device(rhs, blocks, columns, ghost_lists):
    rows = rhs.shape[0]
    ghost = ghost_lists.shape[1] // 2
    send_up = ghost_lists[0, :ghost]
    send_down = ghost_lists[0, ghost:]
    mats = blocks.reshape(rows, NNZ, BS, BS)
    basis = [rhs]
    for j in range(S):
        current = basis[-1]
        boundary = current[send_up]
        lower = shifted(boundary, "space", 1)
        upper = shifted(current[send_down], "space", -1)
        whole = lax.all_gather(current, "sub", axis=0, tiled=True)
        extended = jnp.concatenate([whole, lower, upper], axis=0)
        picked = extended[columns].reshape(rows, NNZ, BS, NRHS)
        nxt = jnp.einsum("rbij,rbjk->rik", mats, picked, preferred_element_type=jnp.float32)
        basis.append(nxt.astype(jnp.bfloat16).reshape(rows, BS * NRHS))
    stack = jnp.stack(basis, axis=1).reshape(rows, S + 1, BS, NRHS)
    partial_value = jnp.einsum("rjia,rkic->jakc", stack, stack, preferred_element_type=jnp.float32)
    gram = lax.psum(partial_value, ("space", "sub"))
    return finish(rhs, stack, gram)


def solution(mesh):
    in_specs = (
        P(("space", "sub"), None),
        P(("space", "sub"), None, None),
        P(("space", "sub"), None),
        P(("space", "sub"), None),
    )
    out_specs = (P(("space", "sub"), None), P(("space", "sub"), None))
    return jax.shard_map(
        on_device, mesh=mesh, in_specs=in_specs, out_specs=out_specs, check_vma=False
    )
```

profile of v0, /device:TPU:0, one launch (start us, length us, event | category | flops | bytes accessed | tf_op | source)
XLA Modules:
  0.0 319.2 jit_solution(4314674499148985406)
XLA Ops:
  7.2 0.7 all-gather.5.cloned.1.call-update
  8.0 0.8 fusion.27
  8.8 1.8 gather_fusion
  10.6 4.9 %collective-permute-start = (bf16[64,1024]{1,0:T(8,128)(2,1)S(1)}, bf16[64,1024]{1,0:T(8,128)(2,1)S(1)}, u32[]{:S(2)}, u32[]{:S(2)}) collective-permute-start(bf16[64,1024]{1,0:T(8,128)(2,1)S(1)} %gather_fusion), channel_id=1, source_target_pairs={{0,4},{4,8},{8,12},{12,16},{16,20},{20,24},{24,28},{1,5},{5,9},{9,... | collective-permute-start | bytes 393224 | tf_op jit(solution)/shard_map/ppermute | solution.py:15
  15.5 1.8 gather_fusion.1
  17.2 1.3 collective-permute-start.1
  19.1 10.9 %copy.27 = bf16[128,7,4096]{0,2,1:T(8,128)(2,1)} copy(bf16[128,7,4096]{2,0,1:T(8,128)(2,1)} %param.5) | data formatting | bytes 14680064 | tf_op args[1]
  30.0 21.2 %copy.29 = bf16[128,7,64,64]{3,2,1,0:T(8,128)(2,1)} copy(bf16[128,7,64,64]{0,3,2,1:T(8,128)(2,1)} %bitcast.114) | data formatting | bytes 14680064 | tf_op jit(solution)/shard_map/reshape | solution.py:39
  51.7 1.0 constant_dynamic-update-slice_fusion.3
  52.8 1.3 pad_maximum_fusion
  54.1 3.6 %gather_fusion.2 = bf16[896,1024]{1,0:T(8,128)(2,1)S(1)} fusion(bf16[640,1024]{1,0:T(8,128)(2,1)S(1)} %pad_maximum_fusion, s32[1024]{0:T(1024)S(1)} %pad_clamp_fusion), kind=kCustom, calls=%fused_computation.2 | custom fusion | bytes 3673600 | tf_op jit(solution)/shard_map/gather | solution.py:48
  57.7 13.8 %reshape.125 = bf16[128,7,64,16]{3,2,1,0:T(8,128)(2,1)} reshape(bf16[896,1024]{1,0:T(8,128)(2,1)S(1)} %gather_fusion.2) | data formatting | bytes 3670016 | tf_op jit(solution)/shard_map/reshape | solution.py:48
  71.5 12.5 %constant_dynamic-update-slice_fusion.2 = (bf16[128,5,64,16]{2,3,0,1:T(8,128)(2,1)}, bf16[128,16,64]{2,1,0:T(8,128)(2,1)S(1)}) fusion(bf16[128,5,64,16]{2,3,0,1:T(8,128)(2,1)} %constant_dynamic-update-slice_fusion.3, bf16[128,7,64,16]{3,2,1,0:T(8,128)(2,1)} %reshape.125, bf16[128,7,64,64]{3,2,1,0:T(8,128)(2,1)} %copy.29), kind=kOutput, calls=%fused_computation.57 | convolution fusion | flops 117571584 | bytes 30146560 | tf_op jit(solution)/shard_map/rbij,rbjk->rik/dot_general | solution.py:49
  84.1 0.6 copy.30
  84.7 0.9 copy.31
  85.6 1.8 gather_fusion.3
  87.4 1.8 gather_fusion.4
  89.2 4.4 %collective-permute-start.2 = (bf16[64,1024]{1,0:T(8,128)(2,1)S(1)}, bf16[64,1024]{1,0:T(8,128)(2,1)S(1)}, u32[]{:S(2)}, u32[]{:S(2)}) collective-permute-start(bf16[64,1024]{1,0:T(8,128)(2,1)S(1)} %gather_fusion.3), channel_id=1, source_target_pairs={{0,4},{4,8},{8,12},{12,16},{16,20},{20,24},{24,28},{1,5},{5,9},{9,... | collective-permute-start | bytes 393224 | tf_op jit(solution)/shard_map/ppermute | solution.py:15
  93.6 1.5 collective-permute-start.3
  95.1 1.0 collective-permute-done.2
  96.1 4.8 %collective-permute-done.3 = bf16[64,1024]{1,0:T(8,128)(2,1)S(1)} collective-permute-done((bf16[64,1024]{1,0:T(8,128)(2,1)S(1)}, bf16[64,1024]{1,0:T(8,128)(2,1)S(1)}, u32[]{:S(2)}, u32[]{:S(2)}) %collective-permute-start.3) | collective-permute-done | bytes 131104 | tf_op jit(solution)/shard_map/ppermute | solution.py:15
  100.8 3.8 %all-gather.7.cloned.1.call-done = bf16[512,1024]{1,0:T(8,128)(2,1)} async-done(((bf16[128,1024]{1,0:T(8,128)(2,1)}), bf16[512,1024]{1,0:T(8,128)(2,1)}) %all-gather.7.cloned.1.call-update) | async-done | bytes 1048592 | tf_op jit(solution)/shard_map/all_gather | solution.py:46
  104.6 1.3 pad_maximum_fusion.1
  106.0 3.6 %gather_fusion.5 = bf16[896,1024]{1,0:T(8,128)(2,1)S(1)} fusion(bf16[640,1024]{1,0:T(8,128)(2,1)S(1)} %pad_maximum_fusion.1, s32[1024]{0:T(1024)S(1)} %pad_clamp_fusion), kind=kCustom, calls=%fused_computation.5 | custom fusion | bytes 3673600 | tf_op jit(solution)/shard_map/gather | solution.py:48
  109.6 13.8 %reshape.128 = bf16[128,7,64,16]{3,2,1,0:T(8,128)(2,1)} reshape(bf16[896,1024]{1,0:T(8,128)(2,1)S(1)} %gather_fusion.5) | data formatting | bytes 3670016 | tf_op jit(solution)/shard_map/reshape | solution.py:48
  123.4 12.5 %constant_dynamic-update-slice_fusion.1 = (bf16[128,5,64,16]{2,3,0,1:T(8,128)(2,1)}, bf16[128,16,64]{2,1,0:T(8,128)(2,1)S(1)}) fusion(bf16[128,5,64,16]{2,3,0,1:T(8,128)(2,1)} %get-tuple-element.8, bf16[128,7,64,16]{3,2,1,0:T(8,128)(2,1)} %reshape.128, bf16[128,7,64,64]{3,2,1,0:T(8,128)(2,1)} %copy.29), kind=kOutput, calls=%fused_computation.56 | convolution fusion | flops 117571584 | bytes 30146560 | tf_op jit(solution)/shard_map/rbij,rbjk->rik/dot_general | solution.py:49
  135.9 0.6 copy.36
  136.5 0.9 copy.37
  137.5 1.8 gather_fusion.6
  139.2 1.8 gather_fusion.7
  141.0 3.4 %collective-permute-start.4 = (bf16[64,1024]{1,0:T(8,128)(2,1)S(1)}, bf16[64,1024]{1,0:T(8,128)(2,1)S(1)}, u32[]{:S(2)}, u32[]{:S(2)}) collective-permute-start(bf16[64,1024]{1,0:T(8,128)(2,1)S(1)} %gather_fusion.6), channel_id=1, source_target_pairs={{0,4},{4,8},{8,12},{12,16},{16,20},{20,24},{24,28},{1,5},{5,9},{9,... | collective-permute-start | bytes 393224 | tf_op jit(solution)/shard_map/ppermute | solution.py:15
  144.4 1.3 collective-permute-start.5
  145.7 1.8 collective-permute-done.4
  147.6 4.1 %collective-permute-done.5 = bf16[64,1024]{1,0:T(8,128)(2,1)S(1)} collective-permute-done((bf16[64,1024]{1,0:T(8,128)(2,1)S(1)}, bf16[64,1024]{1,0:T(8,128)(2,1)S(1)}, u32[]{:S(2)}, u32[]{:S(2)}) %collective-permute-start.5) | collective-permute-done | bytes 131104 | tf_op jit(solution)/shard_map/ppermute | solution.py:15
  151.7 2.6 all-gather.9.cloned.1.call-done
  154.3 1.3 pad_maximum_fusion.2
  155.6 3.6 %gather_fusion.8 = bf16[896,1024]{1,0:T(8,128)(2,1)S(1)} fusion(bf16[640,1024]{1,0:T(8,128)(2,1)S(1)} %pad_maximum_fusion.2, s32[1024]{0:T(1024)S(1)} %pad_clamp_fusion), kind=kCustom, calls=%fused_computation.8 | custom fusion | bytes 3673600 | tf_op jit(solution)/shard_map/gather | solution.py:48
  159.3 13.8 %reshape.130 = bf16[128,7,64,16]{3,2,1,0:T(8,128)(2,1)} reshape(bf16[896,1024]{1,0:T(8,128)(2,1)S(1)} %gather_fusion.8) | data formatting | bytes 3670016 | tf_op jit(solution)/shard_map/reshape | solution.py:48
  173.1 12.5 %constant_dynamic-update-slice_fusion = (bf16[128,5,64,16]{2,3,0,1:T(8,128)(2,1)}, bf16[128,16,64]{2,1,0:T(8,128)(2,1)S(1)}) fusion(bf16[128,5,64,16]{2,3,0,1:T(8,128)(2,1)} %get-tuple-element.10, bf16[128,7,64,16]{3,2,1,0:T(8,128)(2,1)} %reshape.130, bf16[128,7,64,64]{3,2,1,0:T(8,128)(2,1)} %copy.29), kind=kOutput, calls=%fused_computation.55 | convolution fusion | flops 117571584 | bytes 30146560 | tf_op jit(solution)/shard_map/rbij,rbjk->rik/dot_general | solution.py:49
  186.2 0.9 copy.44
  187.1 1.8 gather_fusion.9
  188.9 1.8 gather_fusion.10
  190.6 3.4 %collective-permute-start.6 = (bf16[64,1024]{1,0:T(8,128)(2,1)S(1)}, bf16[64,1024]{1,0:T(8,128)(2,1)S(1)}, u32[]{:S(2)}, u32[]{:S(2)}) collective-permute-start(bf16[64,1024]{1,0:T(8,128)(2,1)S(1)} %gather_fusion.9), channel_id=1, source_target_pairs={{0,4},{4,8},{8,12},{12,16},{16,20},{20,24},{24,28},{1,5},{5,9},{9,... | collective-permute-start | bytes 393224 | tf_op jit(solution)/shard_map/ppermute | solution.py:15
  194.0 1.5 collective-permute-start.7
  195.6 0.9 copy.56
  196.5 0.7 collective-permute-done.6
  197.2 4.1 %collective-permute-done.7 = bf16[64,1024]{1,0:T(8,128)(2,1)S(1)} collective-permute-done((bf16[64,1024]{1,0:T(8,128)(2,1)S(1)}, bf16[64,1024]{1,0:T(8,128)(2,1)S(1)}, u32[]{:S(2)}, u32[]{:S(2)}) %collective-permute-start.7) | collective-permute-done | bytes 131104 | tf_op jit(solution)/shard_map/ppermute | solution.py:15
  201.3 2.7 all-gather.11.cloned.1.call-done
  204.0 1.3 pad_maximum_fusion.3
  205.3 3.6 %gather_fusion.11 = bf16[896,1024]{1,0:T(8,128)(2,1)S(1)} fusion(bf16[640,1024]{1,0:T(8,128)(2,1)S(1)} %pad_maximum_fusion.3, s32[1024]{0:T(1024)S(1)} %pad_clamp_fusion), kind=kCustom, calls=%fused_computation.11 | custom fusion | bytes 3673600 | tf_op jit(solution)/shard_map/gather | solution.py:48
  208.9 13.8 %reshape.132 = bf16[128,7,64,16]{3,2,1,0:T(8,128)(2,1)} reshape(bf16[896,1024]{1,0:T(8,128)(2,1)S(1)} %gather_fusion.11) | data formatting | bytes 3670016 | tf_op jit(solution)/shard_map/reshape | solution.py:48
  222.7 12.5 %fusion.18 = bf16[128,5,64,16]{2,3,0,1:T(8,128)(2,1)} fusion(bf16[128,5,64,16]{2,3,0,1:T(8,128)(2,1)} %get-tuple-element.12, bf16[128,7,64,16]{3,2,1,0:T(8,128)(2,1)} %reshape.132, bf16[128,7,64,64]{3,2,1,0:T(8,128)(2,1)} %copy.29), kind=kOutput, calls=%fused_computation.39 | convolution fusion | flops 117571584 | bytes 29884416 | tf_op jit(solution)/shard_map/rbij,rbjk->rik/dot_general | solution.py:49
  235.3 4.7 %convert_element_type.36 = f32[128,5,64,16]{2,3,0,1:T(8,128)} convert(bf16[128,5,64,16]{2,3,0,1:T(8,128)(2,1)} %fusion.18) | non-fusion elementwise | flops 655360 | bytes 3932160 | tf_op jit(solution)/shard_map/convert_element_type | solution.py:25
  240.0 3.8 %fusion.19 = f32[5,16,5,16]{3,1,2,0:T(8,128)S(1)} fusion(bf16[128,5,64,16]{2,3,0,1:T(8,128)(2,1)S(1)} %copy-done.1), kind=kOutput, calls=%fused_computation.40 | convolution fusion | flops 104857600 | bytes 1336320 | tf_op jit(solution)/shard_map/rjia,rkic->jakc/dot_general | solution.py:52
  243.8 43.3 %psum.7 = f32[5,16,5,16]{3,1,2,0:T(8,128)S(1)} all-reduce(f32[5,16,5,16]{3,1,2,0:T(8,128)S(1)} %fusion.19), channel_id=1, replica_groups=mesh['space'=8,'sub'=4] {'space','sub'}, use_global_device_ids=true, to_apply=%region_0.0 | all-reduce | flops 6400 | bytes 51200 | tf_op jit(solution)/shard_map/psum | solution.py:53
  287.5 5.8 %cholesky.16 = f32[64,64]{1,0:T(8,128)S(1)} custom-call(f32[64,64]{1,0:T(8,128)S(1)} %fusion.26), custom_call_target="Cholesky" | custom-call | tf_op jit(solution)/shard_map/jit(cholesky)/cholesky | solution.py:23
  293.4 0.7 compare_reduce_fusion
  294.6 4.9 %custom-call.10 = f32[1,64,64]{1,2,0:T(8,128)S(1)} custom-call(f32[1,64,64]{2,1,0:T(8,128)S(1)} %fusion.24), custom_call_target="InvertDiagBlocksLowerTriangular" | custom-call | tf_op jit(solution)/shard_map/jit(_cho_solve)/triangular_solve | solution.py:24
  300.1 4.8 %fusion = f32[128,64,16,1]{1,2,0,3:T(8,128)S(1)} fusion(f32[4,16,16,1]{1,2,3,0:T(8,128)S(1)} %convolution_bitcast_fusion.4, f32[128,5,64,16]{2,3,0,1:T(8,128)} %convert_element_type.36), kind=kOutput, calls=%fused_computation.13 | convolution fusion | flops 101187584 | bytes 8916992 | tf_op jit(solution)/shard_map/rjia,jac->ric/dot_general | solution.py:29
  305.5 1.2 bitcast_subtract_fusion
  306.7 1.0 copy.60
  307.7 2.2 fusion.5
  309.9 1.7 copy.75
  311.6 1.0 copy.59
  (53 shorter events, 4.0 us)
Async XLA Ops:
  7.2 11.7 %copy-start = (bf16[128,1024]{1,0:T(8,128)(2,1)S(1)}, bf16[128,1024]{1,0:T(8,128)(2,1)}, u32[]{:S(2)}) copy-start(bf16[128,1024]{1,0:T(8,128)(2,1)} %param.4) | copy-start | bytes 786436
  7.2 11.4 %copy-start.10 = (s32[128,7]{0,1:T(8,128)S(1)}, s32[128,7]{0,1:T(8,128)}, u32[]{:S(2)}) copy-start(s32[128,7]{0,1:T(8,128)} %param.6) | copy-start | bytes 10756
  7.2 45.6 %all-gather.5.cloned.1.call-start = ((), (), s32[]{:S(2)}) async-start(), calls=%async_computation | async-start | bytes 1310720 | tf_op jit(solution)/shard_map/all_gather | solution.py:46
  7.9 96.7 %all-gather.7.cloned.1.call-start = ((), (), s32[]{:S(2)}) async-start(), calls=%async_computation.1 | async-start | bytes 1310720 | tf_op jit(solution)/shard_map/all_gather | solution.py:46
  10.6 42.1 %collective-permute-start = (bf16[64,1024]{1,0:T(8,128)(2,1)S(1)}, bf16[64,1024]{1,0:T(8,128)(2,1)S(1)}, u32[]{:S(2)}, u32[]{:S(2)}) collective-permute-start(bf16[64,1024]{1,0:T(8,128)(2,1)S(1)} %gather_fusion), channel_id=1, source_target_pairs={{0,4},{4,8},{8,12},{12,16},{16,20},{20,24},{24,28},{1,5},{5,9},{9,... | collective-permute-start | bytes 393224 | tf_op jit(solution)/shard_map/ppermute | solution.py:15
  17.2 35.5 %collective-permute-start.1 = (bf16[64,1024]{1,0:T(8,128)(2,1)S(1)}, bf16[64,1024]{1,0:T(8,128)(2,1)S(1)}, u32[]{:S(2)}, u32[]{:S(2)}) collective-permute-start(bf16[64,1024]{1,0:T(8,128)(2,1)S(1)} %gather_fusion.1), channel_id=1, source_target_pairs={{4,0},{8,4},{12,8},{16,12},{20,16},{24,20},{28,24},{5,1},{9,5},{13... | collective-permute-start | bytes 393224 | tf_op jit(solution)/shard_map/ppermute | solution.py:15
  51.7 1.0 copy-start.8
  84.1 16.8 %copy-start.2 = (bf16[128,16,64]{2,1,0:T(8,128)(2,1)}, bf16[128,16,64]{2,1,0:T(8,128)(2,1)S(1)}, u32[]{:S(2)}) copy-start(bf16[128,16,64]{2,1,0:T(8,128)(2,1)S(1)} %get-tuple-element.9) | copy-start | bytes 786436
  85.5 68.8 %all-gather.9.cloned.1.call-start = ((), (), s32[]{:S(2)}) async-start(), calls=%async_computation.2 | async-start | bytes 1310720 | tf_op jit(solution)/shard_map/all_gather | solution.py:46
  89.2 6.9 %collective-permute-start.2 = (bf16[64,1024]{1,0:T(8,128)(2,1)S(1)}, bf16[64,1024]{1,0:T(8,128)(2,1)S(1)}, u32[]{:S(2)}, u32[]{:S(2)}) collective-permute-start(bf16[64,1024]{1,0:T(8,128)(2,1)S(1)} %gather_fusion.3), channel_id=1, source_target_pairs={{0,4},{4,8},{8,12},{12,16},{16,20},{20,24},{24,28},{1,5},{5,9},{9,... | collective-permute-start | bytes 393224 | tf_op jit(solution)/shard_map/ppermute | solution.py:15
  93.6 7.3 %collective-permute-start.3 = (bf16[64,1024]{1,0:T(8,128)(2,1)S(1)}, bf16[64,1024]{1,0:T(8,128)(2,1)S(1)}, u32[]{:S(2)}, u32[]{:S(2)}) collective-permute-start(bf16[64,1024]{1,0:T(8,128)(2,1)S(1)} %gather_fusion.4), channel_id=1, source_target_pairs={{4,0},{8,4},{12,8},{16,12},{20,16},{24,20},{28,24},{5,1},{9,5},{13... | collective-permute-start | bytes 393224 | tf_op jit(solution)/shard_map/ppermute | solution.py:15
  135.9 15.7 %copy-start.4 = (bf16[128,16,64]{2,1,0:T(8,128)(2,1)}, bf16[128,16,64]{2,1,0:T(8,128)(2,1)S(1)}, u32[]{:S(2)}) copy-start(bf16[128,16,64]{2,1,0:T(8,128)(2,1)S(1)} %get-tuple-element.11) | copy-start | bytes 786436
  137.4 66.5 %all-gather.11.cloned.1.call-start = ((), (), s32[]{:S(2)}) async-start(), calls=%async_computation.3 | async-start | bytes 1310720 | tf_op jit(solution)/shard_map/all_gather | solution.py:46
  141.0 6.5 %collective-permute-start.4 = (bf16[64,1024]{1,0:T(8,128)(2,1)S(1)}, bf16[64,1024]{1,0:T(8,128)(2,1)S(1)}, u32[]{:S(2)}, u32[]{:S(2)}) collective-permute-start(bf16[64,1024]{1,0:T(8,128)(2,1)S(1)} %gather_fusion.6), channel_id=1, source_target_pairs={{0,4},{4,8},{8,12},{12,16},{16,20},{20,24},{24,28},{1,5},{5,9},{9,... | collective-permute-start | bytes 393224 | tf_op jit(solution)/shard_map/ppermute | solution.py:15
  144.4 7.2 %collective-permute-start.5 = (bf16[64,1024]{1,0:T(8,128)(2,1)S(1)}, bf16[64,1024]{1,0:T(8,128)(2,1)S(1)}, u32[]{:S(2)}, u32[]{:S(2)}) collective-permute-start(bf16[64,1024]{1,0:T(8,128)(2,1)S(1)} %gather_fusion.7), channel_id=1, source_target_pairs={{4,0},{8,4},{12,8},{16,12},{20,16},{24,20},{28,24},{5,1},{9,5},{13... | collective-permute-start | bytes 393224 | tf_op jit(solution)/shard_map/ppermute | solution.py:15
  185.6 15.7 %copy-start.6 = (bf16[128,16,64]{2,1,0:T(8,128)(2,1)}, bf16[128,16,64]{2,1,0:T(8,128)(2,1)S(1)}, u32[]{:S(2)}) copy-start(bf16[128,16,64]{2,1,0:T(8,128)(2,1)S(1)} %get-tuple-element.13) | copy-start | bytes 786436
  190.6 6.5 %collective-permute-start.6 = (bf16[64,1024]{1,0:T(8,128)(2,1)S(1)}, bf16[64,1024]{1,0:T(8,128)(2,1)S(1)}, u32[]{:S(2)}, u32[]{:S(2)}) collective-permute-start(bf16[64,1024]{1,0:T(8,128)(2,1)S(1)} %gather_fusion.9), channel_id=1, source_target_pairs={{0,4},{4,8},{8,12},{12,16},{16,20},{20,24},{24,28},{1,5},{5,9},{9,... | collective-permute-start | bytes 393224 | tf_op jit(solution)/shard_map/ppermute | solution.py:15
  194.0 7.2 %collective-permute-start.7 = (bf16[64,1024]{1,0:T(8,128)(2,1)S(1)}, bf16[64,1024]{1,0:T(8,128)(2,1)S(1)}, u32[]{:S(2)}, u32[]{:S(2)}) collective-permute-start(bf16[64,1024]{1,0:T(8,128)(2,1)S(1)} %gather_fusion.10), channel_id=1, source_target_pairs={{4,0},{8,4},{12,8},{16,12},{20,16},{24,20},{28,24},{5,1},{9,5},{13... | collective-permute-start | bytes 393224 | tf_op jit(solution)/shard_map/ppermute | solution.py:15
  235.3 4.7 %copy-start.1 = (bf16[128,5,64,16]{2,3,0,1:T(8,128)(2,1)S(1)}, bf16[128,5,64,16]{2,3,0,1:T(8,128)(2,1)}, u32[]{:S(2)}) copy-start(bf16[128,5,64,16]{2,3,0,1:T(8,128)(2,1)} %fusion.18) | copy-start | bytes 3932164
  304.9 2.8 copy-start.3
  304.9 2.8 copy-start.5
  304.9 2.8 copy-start.7
  305.5 2.2 copy-start.9
Sparse Core Ops, SparseCore 0:
  9.6 19.4 all-gather.4
  85.6 18.9 all-gather.6
  137.5 16.7 all-gather.8
  187.2 16.7 all-gather.10
where the time goes:
time: 321 us; the launch traced here: 319 us
  local copies, waits for them, and re-layouts  128 us (40%)
  matrix products  61.5 us (19%)
  blocking collectives  43.3 us (13%)
  waiting for transfers between devices  26.3 us (8%)
  other arithmetic  24.1 us (8%)
  starting transfers between devices  21.8 us (7%)
  between operations  14.2 us (4%)
    reshape x4, local copies, waits for them, and re-layouts, on_device(): picked = extended[columns].reshape(rows, NNZ, BS, NRHS)  55.2 us
    dot_general x4, matrix products, on_device(): jnp.einsum('rbij,rbjk->rik', mats, picked, preferred_element_type=jnp.flo...  50.1 us
    psum x1, blocking collectives, on_device(): gram = lax.psum(partial_value, ('space', 'sub'))  43.3 us
    ppermute x8, starting transfers between devices, shifted(): lax.ppermute(value, axis, [(source, source + steps) for source in range(i...  21.6 us
    reshape x1, local copies, waits for them, and re-layouts, on_device(): mats = blocks.reshape(rows, NNZ, BS, BS)  21.2 us
    ppermute x8, waiting for transfers between devices, shifted(): lax.ppermute(value, axis, [(source, source + steps) for source in range(i...  16.5 us
    gather x4, local copies, waits for them, and re-layouts, on_device(): picked = extended[columns].reshape(rows, NNZ, BS, NRHS)  14.4 us
    unnamed x27, local copies, waits for them, and re-layouts  14.1 us
  transfers between devices with their start and end apart: 12, of which 9 were waited for; matrix products, arithmetic and copies ran while one was open for 16% of the time, Pallas kernels for 0%

commit v1 on v0

--- a/solution.py
+++ b/solution.py
@@ -50,7 +50,7 @@
         basis.append(nxt.astype(jnp.bfloat16).reshape(rows, BS * NRHS))
     stack = jnp.stack(basis, axis=1).reshape(rows, S + 1, BS, NRHS)
     partial_value = jnp.einsum("rjia,rkic->jakc", stack, stack, preferred_element_type=jnp.float32)
-    gram = lax.psum(partial_value, ("space", "sub"))
+    gram = lax.psum(lax.psum(partial_value, "sub"), "space")
     return finish(rhs, stack, gram)
 
 

time: 321 us -> 330 us (1.028)
  blocking collectives: 43.3 us -> 53.2 us
    psum x1 -> x2, blocking collectives: 43.3 us -> 53.2 us  [on_device(): gram = lax.psum(lax.psum(partial_value, 'sub'), 'space')]
  transfers between devices with their start and end apart: 12 -> 12, of which waited for: 9 -> 9; matrix products, arithmetic and copies ran while one was open for 16% -> 15% of each run, Pallas kernels for 0% -> 0%
where the time goes in v1:
time: 330 us; the launch traced here: 329 us
  local copies, waits for them, and re-layouts  128 us (39%)
  matrix products  61.5 us (19%)
  blocking collectives  53.2 us (16%)
  waiting for transfers between devices  26.3 us (8%)
  other arithmetic  24.3 us (7%)
  starting transfers between devices  21.8 us (7%)
  between operations  14.2 us (4%)
    reshape x4, local copies, waits for them, and re-layouts, on_device(): picked = extended[columns].reshape(rows, NNZ, BS, NRHS)  54.9 us
    psum x2, blocking collectives, on_device(): gram = lax.psum(lax.psum(partial_value, 'sub'), 'space')  53.2 us
    dot_general x4, matrix products, on_device(): jnp.einsum('rbij,rbjk->rik', mats, picked, preferred_element_type=jnp.flo...  50.1 us
    ppermute x8, starting transfers between devices, shifted(): lax.ppermute(value, axis, [(source, source + steps) for source in range(i...  21.6 us
    reshape x1, local copies, waits for them, and re-layouts, on_device(): mats = blocks.reshape(rows, NNZ, BS, BS)  21.2 us
    ppermute x8, waiting for transfers between devices, shifted(): lax.ppermute(value, axis, [(source, source + steps) for source in range(i...  16.5 us
    gather x4, local copies, waits for them, and re-layouts, on_device(): picked = extended[columns].reshape(rows, NNZ, BS, NRHS)  14.4 us
    unnamed x27, local copies, waits for them, and re-layouts  14.1 us
  transfers between devices with their start and end apart: 12, of which 9 were waited for; matrix products, arithmetic and copies ran while one was open for 15% of the time, Pallas kernels for 0%

profile of v1, /device:TPU:0, one launch (start us, length us, event | category | flops | bytes accessed | tf_op | source)
XLA Modules:
  0.0 329.0 jit_solution(17564537248717988769)
XLA Ops:
  7.2 0.7 all-gather.5.cloned.1.call-update
  8.0 0.8 fusion.27
  8.8 1.8 gather_fusion
  10.6 4.9 %collective-permute-start = (bf16[64,1024]{1,0:T(8,128)(2,1)S(1)}, bf16[64,1024]{1,0:T(8,128)(2,1)S(1)}, u32[]{:S(2)}, u32[]{:S(2)}) collective-permute-start(bf16[64,1024]{1,0:T(8,128)(2,1)S(1)} %gather_fusion), channel_id=1, source_target_pairs={{0,4},{4,8},{8,12},{12,16},{16,20},{20,24},{24,28},{1,5},{5,9},{9,... | collective-permute-start | bytes 393224 | tf_op jit(solution)/shard_map/ppermute | solution.py:15
  15.5 1.8 gather_fusion.1
  17.2 1.3 collective-permute-start.1
  19.1 10.9 %copy.27 = bf16[128,7,4096]{0,2,1:T(8,128)(2,1)} copy(bf16[128,7,4096]{2,0,1:T(8,128)(2,1)} %param.5) | data formatting | bytes 14680064 | tf_op args[1]
  30.0 21.2 %copy.29 = bf16[128,7,64,64]{3,2,1,0:T(8,128)(2,1)} copy(bf16[128,7,64,64]{0,3,2,1:T(8,128)(2,1)} %bitcast.114) | data formatting | bytes 14680064 | tf_op jit(solution)/shard_map/reshape | solution.py:39
  51.8 0.9 constant_dynamic-update-slice_fusion.3
  52.8 1.3 pad_maximum_fusion
  54.1 3.6 %gather_fusion.2 = bf16[896,1024]{1,0:T(8,128)(2,1)S(1)} fusion(bf16[640,1024]{1,0:T(8,128)(2,1)S(1)} %pad_maximum_fusion, s32[1024]{0:T(1024)S(1)} %pad_clamp_fusion), kind=kCustom, calls=%fused_computation.2 | custom fusion | bytes 3673600 | tf_op jit(solution)/shard_map/gather | solution.py:48
  57.8 13.7 %reshape.125 = bf16[128,7,64,16]{3,2,1,0:T(8,128)(2,1)} reshape(bf16[896,1024]{1,0:T(8,128)(2,1)S(1)} %gather_fusion.2) | data formatting | bytes 3670016 | tf_op jit(solution)/shard_map/reshape | solution.py:48
  71.5 12.5 %constant_dynamic-update-slice_fusion.2 = (bf16[128,5,64,16]{2,3,0,1:T(8,128)(2,1)}, bf16[128,16,64]{2,1,0:T(8,128)(2,1)S(1)}) fusion(bf16[128,5,64,16]{2,3,0,1:T(8,128)(2,1)} %constant_dynamic-update-slice_fusion.3, bf16[128,7,64,16]{3,2,1,0:T(8,128)(2,1)} %reshape.125, bf16[128,7,64,64]{3,2,1,0:T(8,128)(2,1)} %copy.29), kind=kOutput, calls=%fused_computation.57 | convolution fusion | flops 117571584 | bytes 30146560 | tf_op jit(solution)/shard_map/rbij,rbjk->rik/dot_general | solution.py:49
  84.6 0.9 copy.31
  85.5 1.8 gather_fusion.3
  87.3 1.8 gather_fusion.4
  89.1 4.4 %collective-permute-start.2 = (bf16[64,1024]{1,0:T(8,128)(2,1)S(1)}, bf16[64,1024]{1,0:T(8,128)(2,1)S(1)}, u32[]{:S(2)}, u32[]{:S(2)}) collective-permute-start(bf16[64,1024]{1,0:T(8,128)(2,1)S(1)} %gather_fusion.3), channel_id=1, source_target_pairs={{0,4},{4,8},{8,12},{12,16},{16,20},{20,24},{24,28},{1,5},{5,9},{9,... | collective-permute-start | bytes 393224 | tf_op jit(solution)/shard_map/ppermute | solution.py:15
  93.5 1.5 collective-permute-start.3
  95.0 1.0 collective-permute-done.2
  96.0 4.8 %collective-permute-done.3 = bf16[64,1024]{1,0:T(8,128)(2,1)S(1)} collective-permute-done((bf16[64,1024]{1,0:T(8,128)(2,1)S(1)}, bf16[64,1024]{1,0:T(8,128)(2,1)S(1)}, u32[]{:S(2)}, u32[]{:S(2)}) %collective-permute-start.3) | collective-permute-done | bytes 131104 | tf_op jit(solution)/shard_map/ppermute | solution.py:15
  100.8 3.8 %all-gather.7.cloned.1.call-done = bf16[512,1024]{1,0:T(8,128)(2,1)} async-done(((bf16[128,1024]{1,0:T(8,128)(2,1)}), bf16[512,1024]{1,0:T(8,128)(2,1)}) %all-gather.7.cloned.1.call-update) | async-done | bytes 1048592 | tf_op jit(solution)/shard_map/all_gather | solution.py:46
  104.6 1.3 pad_maximum_fusion.1
  105.9 3.6 %gather_fusion.5 = bf16[896,1024]{1,0:T(8,128)(2,1)S(1)} fusion(bf16[640,1024]{1,0:T(8,128)(2,1)S(1)} %pad_maximum_fusion.1, s32[1024]{0:T(1024)S(1)} %pad_clamp_fusion), kind=kCustom, calls=%fused_computation.5 | custom fusion | bytes 3673600 | tf_op jit(solution)/shard_map/gather | solution.py:48
  109.6 13.7 %reshape.128 = bf16[128,7,64,16]{3,2,1,0:T(8,128)(2,1)} reshape(bf16[896,1024]{1,0:T(8,128)(2,1)S(1)} %gather_fusion.5) | data formatting | bytes 3670016 | tf_op jit(solution)/shard_map/reshape | solution.py:48
  123.3 12.5 %constant_dynamic-update-slice_fusion.1 = (bf16[128,5,64,16]{2,3,0,1:T(8,128)(2,1)}, bf16[128,16,64]{2,1,0:T(8,128)(2,1)S(1)}) fusion(bf16[128,5,64,16]{2,3,0,1:T(8,128)(2,1)} %get-tuple-element.8, bf16[128,7,64,16]{3,2,1,0:T(8,128)(2,1)} %reshape.128, bf16[128,7,64,64]{3,2,1,0:T(8,128)(2,1)} %copy.29), kind=kOutput, calls=%fused_computation.56 | convolution fusion | flops 117571584 | bytes 30146560 | tf_op jit(solution)/shard_map/rbij,rbjk->rik/dot_general | solution.py:49
  136.4 0.9 copy.37
  137.3 1.8 gather_fusion.6
  139.1 1.8 gather_fusion.7
  140.9 3.4 %collective-permute-start.4 = (bf16[64,1024]{1,0:T(8,128)(2,1)S(1)}, bf16[64,1024]{1,0:T(8,128)(2,1)S(1)}, u32[]{:S(2)}, u32[]{:S(2)}) collective-permute-start(bf16[64,1024]{1,0:T(8,128)(2,1)S(1)} %gather_fusion.6), channel_id=1, source_target_pairs={{0,4},{4,8},{8,12},{12,16},{16,20},{20,24},{24,28},{1,5},{5,9},{9,... | collective-permute-start | bytes 393224 | tf_op jit(solution)/shard_map/ppermute | solution.py:15
  144.3 1.3 collective-permute-start.5
  145.6 1.8 collective-permute-done.4
  147.4 4.1 %collective-permute-done.5 = bf16[64,1024]{1,0:T(8,128)(2,1)S(1)} collective-permute-done((bf16[64,1024]{1,0:T(8,128)(2,1)S(1)}, bf16[64,1024]{1,0:T(8,128)(2,1)S(1)}, u32[]{:S(2)}, u32[]{:S(2)}) %collective-permute-start.5) | collective-permute-done | bytes 131104 | tf_op jit(solution)/shard_map/ppermute | solution.py:15
  151.5 2.6 all-gather.9.cloned.1.call-done
  154.1 1.3 pad_maximum_fusion.2
  155.5 3.6 %gather_fusion.8 = bf16[896,1024]{1,0:T(8,128)(2,1)S(1)} fusion(bf16[640,1024]{1,0:T(8,128)(2,1)S(1)} %pad_maximum_fusion.2, s32[1024]{0:T(1024)S(1)} %pad_clamp_fusion), kind=kCustom, calls=%fused_computation.8 | custom fusion | bytes 3673600 | tf_op jit(solution)/shard_map/gather | solution.py:48
  159.1 13.7 %reshape.130 = bf16[128,7,64,16]{3,2,1,0:T(8,128)(2,1)} reshape(bf16[896,1024]{1,0:T(8,128)(2,1)S(1)} %gather_fusion.8) | data formatting | bytes 3670016 | tf_op jit(solution)/shard_map/reshape | solution.py:48
  172.8 12.5 %constant_dynamic-update-slice_fusion = (bf16[128,5,64,16]{2,3,0,1:T(8,128)(2,1)}, bf16[128,16,64]{2,1,0:T(8,128)(2,1)S(1)}) fusion(bf16[128,5,64,16]{2,3,0,1:T(8,128)(2,1)} %get-tuple-element.10, bf16[128,7,64,16]{3,2,1,0:T(8,128)(2,1)} %reshape.130, bf16[128,7,64,64]{3,2,1,0:T(8,128)(2,1)} %copy.29), kind=kOutput, calls=%fused_computation.55 | convolution fusion | flops 117571584 | bytes 30146560 | tf_op jit(solution)/shard_map/rbij,rbjk->rik/dot_general | solution.py:49
  186.0 0.8 copy.44
  186.8 1.8 gather_fusion.9
  188.6 1.8 gather_fusion.10
  190.4 3.4 %collective-permute-start.6 = (bf16[64,1024]{1,0:T(8,128)(2,1)S(1)}, bf16[64,1024]{1,0:T(8,128)(2,1)S(1)}, u32[]{:S(2)}, u32[]{:S(2)}) collective-permute-start(bf16[64,1024]{1,0:T(8,128)(2,1)S(1)} %gather_fusion.9), channel_id=1, source_target_pairs={{0,4},{4,8},{8,12},{12,16},{16,20},{20,24},{24,28},{1,5},{5,9},{9,... | collective-permute-start | bytes 393224 | tf_op jit(solution)/shard_map/ppermute | solution.py:15
  193.8 1.5 collective-permute-start.7
  195.3 0.9 copy.56
  196.3 0.7 collective-permute-done.6
  196.9 4.1 %collective-permute-done.7 = bf16[64,1024]{1,0:T(8,128)(2,1)S(1)} collective-permute-done((bf16[64,1024]{1,0:T(8,128)(2,1)S(1)}, bf16[64,1024]{1,0:T(8,128)(2,1)S(1)}, u32[]{:S(2)}, u32[]{:S(2)}) %collective-permute-start.7) | collective-permute-done | bytes 131104 | tf_op jit(solution)/shard_map/ppermute | solution.py:15
  201.1 2.7 all-gather.11.cloned.1.call-done
  203.7 1.3 pad_maximum_fusion.3
  205.1 3.6 %gather_fusion.11 = bf16[896,1024]{1,0:T(8,128)(2,1)S(1)} fusion(bf16[640,1024]{1,0:T(8,128)(2,1)S(1)} %pad_maximum_fusion.3, s32[1024]{0:T(1024)S(1)} %pad_clamp_fusion), kind=kCustom, calls=%fused_computation.11 | custom fusion | bytes 3673600 | tf_op jit(solution)/shard_map/gather | solution.py:48
  208.7 13.7 %reshape.132 = bf16[128,7,64,16]{3,2,1,0:T(8,128)(2,1)} reshape(bf16[896,1024]{1,0:T(8,128)(2,1)S(1)} %gather_fusion.11) | data formatting | bytes 3670016 | tf_op jit(solution)/shard_map/reshape | solution.py:48
  222.4 12.5 %fusion.18 = bf16[128,5,64,16]{2,3,0,1:T(8,128)(2,1)} fusion(bf16[128,5,64,16]{2,3,0,1:T(8,128)(2,1)} %get-tuple-element.12, bf16[128,7,64,16]{3,2,1,0:T(8,128)(2,1)} %reshape.132, bf16[128,7,64,64]{3,2,1,0:T(8,128)(2,1)} %copy.29), kind=kOutput, calls=%fused_computation.39 | convolution fusion | flops 117571584 | bytes 29884416 | tf_op jit(solution)/shard_map/rbij,rbjk->rik/dot_general | solution.py:49
  234.9 4.7 %convert_element_type.36 = f32[128,5,64,16]{2,3,0,1:T(8,128)} convert(bf16[128,5,64,16]{2,3,0,1:T(8,128)(2,1)} %fusion.18) | non-fusion elementwise | flops 655360 | bytes 3932160 | tf_op jit(solution)/shard_map/convert_element_type | solution.py:25
  239.6 3.8 %fusion.19 = f32[5,16,5,16]{3,1,2,0:T(8,128)S(1)} fusion(bf16[128,5,64,16]{2,3,0,1:T(8,128)(2,1)S(1)} %copy-done.1), kind=kOutput, calls=%fused_computation.40 | convolution fusion | flops 104857600 | bytes 1336320 | tf_op jit(solution)/shard_map/rjia,rkic->jakc/dot_general | solution.py:52
  243.5 12.7 %psum.14 = f32[5,16,5,16]{3,1,2,0:T(8,128)S(1)} all-reduce(f32[5,16,5,16]{3,1,2,0:T(8,128)S(1)} %fusion.19), channel_id=1, replica_groups=mesh['space'=8,'sub'=4] {'sub'}, use_global_device_ids=true, to_apply=%region_0.0 | all-reduce | flops 6400 | bytes 51200 | tf_op jit(solution)/shard_map/psum | solution.py:53
  256.2 40.5 %psum.15 = f32[5,16,5,16]{3,1,2,0:T(8,128)S(1)} all-reduce(f32[5,16,5,16]{3,1,2,0:T(8,128)S(1)} %psum.14), channel_id=1, replica_groups=mesh['space'=8,'sub'=4] {'space'}, use_global_device_ids=true, to_apply=%region_1.0 | all-reduce | flops 6400 | bytes 51200 | tf_op jit(solution)/shard_map/psum | solution.py:53
  297.1 5.8 %cholesky.16 = f32[64,64]{1,0:T(8,128)S(1)} custom-call(f32[64,64]{1,0:T(8,128)S(1)} %fusion.26), custom_call_target="Cholesky" | custom-call | tf_op jit(solution)/shard_map/jit(cholesky)/cholesky | solution.py:23
  303.0 0.7 compare_reduce_fusion
  303.7 0.7 fusion.24
  304.4 4.9 %custom-call.10 = f32[1,64,64]{1,2,0:T(8,128)S(1)} custom-call(f32[1,64,64]{2,1,0:T(8,128)S(1)} %fusion.24), custom_call_target="InvertDiagBlocksLowerTriangular" | custom-call | tf_op jit(solution)/shard_map/jit(_cho_solve)/triangular_solve | solution.py:24
  309.9 4.8 %fusion = f32[128,64,16,1]{1,2,0,3:T(8,128)S(1)} fusion(f32[4,16,16,1]{1,2,3,0:T(8,128)S(1)} %convolution_bitcast_fusion.4, f32[128,5,64,16]{2,3,0,1:T(8,128)} %convert_element_type.36), kind=kOutput, calls=%fused_computation.13 | convolution fusion | flops 101187584 | bytes 8916992 | tf_op jit(solution)/shard_map/rjia,jac->ric/dot_general | solution.py:29
  315.3 1.2 bitcast_subtract_fusion
  316.5 1.0 copy.60
  317.5 2.2 fusion.5
  319.7 1.7 copy.75
  321.4 1.0 copy.59
  (54 shorter events, 4.6 us)
Async XLA Ops:
  7.2 11.7 %copy-start = (bf16[128,1024]{1,0:T(8,128)(2,1)S(1)}, bf16[128,1024]{1,0:T(8,128)(2,1)}, u32[]{:S(2)}) copy-start(bf16[128,1024]{1,0:T(8,128)(2,1)} %param.4) | copy-start | bytes 786436
  7.2 11.4 %copy-start.10 = (s32[128,7]{0,1:T(8,128)S(1)}, s32[128,7]{0,1:T(8,128)}, u32[]{:S(2)}) copy-start(s32[128,7]{0,1:T(8,128)} %param.6) | copy-start | bytes 10756
  7.2 45.6 %all-gather.5.cloned.1.call-start = ((), (), s32[]{:S(2)}) async-start(), calls=%async_computation | async-start | bytes 1310720 | tf_op jit(solution)/shard_map/all_gather | solution.py:46
  7.9 96.7 %all-gather.7.cloned.1.call-start = ((), (), s32[]{:S(2)}) async-start(), calls=%async_computation.1 | async-start | bytes 1310720 | tf_op jit(solution)/shard_map/all_gather | solution.py:46
  10.6 42.1 %collective-permute-start = (bf16[64,1024]{1,0:T(8,128)(2,1)S(1)}, bf16[64,1024]{1,0:T(8,128)(2,1)S(1)}, u32[]{:S(2)}, u32[]{:S(2)}) collective-permute-start(bf16[64,1024]{1,0:T(8,128)(2,1)S(1)} %gather_fusion), channel_id=1, source_target_pairs={{0,4},{4,8},{8,12},{12,16},{16,20},{20,24},{24,28},{1,5},{5,9},{9,... | collective-permute-start | bytes 393224 | tf_op jit(solution)/shard_map/ppermute | solution.py:15
  17.2 35.5 %collective-permute-start.1 = (bf16[64,1024]{1,0:T(8,128)(2,1)S(1)}, bf16[64,1024]{1,0:T(8,128)(2,1)S(1)}, u32[]{:S(2)}, u32[]{:S(2)}) collective-permute-start(bf16[64,1024]{1,0:T(8,128)(2,1)S(1)} %gather_fusion.1), channel_id=1, source_target_pairs={{4,0},{8,4},{12,8},{16,12},{20,16},{24,20},{28,24},{5,1},{9,5},{13... | collective-permute-start | bytes 393224 | tf_op jit(solution)/shard_map/ppermute | solution.py:15
  51.8 1.0 copy-start.8
  84.0 16.8 %copy-start.2 = (bf16[128,16,64]{2,1,0:T(8,128)(2,1)}, bf16[128,16,64]{2,1,0:T(8,128)(2,1)S(1)}, u32[]{:S(2)}) copy-start(bf16[128,16,64]{2,1,0:T(8,128)(2,1)S(1)} %get-tuple-element.9) | copy-start | bytes 786436
  85.5 68.7 %all-gather.9.cloned.1.call-start = ((), (), s32[]{:S(2)}) async-start(), calls=%async_computation.2 | async-start | bytes 1310720 | tf_op jit(solution)/shard_map/all_gather | solution.py:46
  89.1 6.9 %collective-permute-start.2 = (bf16[64,1024]{1,0:T(8,128)(2,1)S(1)}, bf16[64,1024]{1,0:T(8,128)(2,1)S(1)}, u32[]{:S(2)}, u32[]{:S(2)}) collective-permute-start(bf16[64,1024]{1,0:T(8,128)(2,1)S(1)} %gather_fusion.3), channel_id=1, source_target_pairs={{0,4},{4,8},{8,12},{12,16},{16,20},{20,24},{24,28},{1,5},{5,9},{9,... | collective-permute-start | bytes 393224 | tf_op jit(solution)/shard_map/ppermute | solution.py:15
  93.5 7.3 %collective-permute-start.3 = (bf16[64,1024]{1,0:T(8,128)(2,1)S(1)}, bf16[64,1024]{1,0:T(8,128)(2,1)S(1)}, u32[]{:S(2)}, u32[]{:S(2)}) collective-permute-start(bf16[64,1024]{1,0:T(8,128)(2,1)S(1)} %gather_fusion.4), channel_id=1, source_target_pairs={{4,0},{8,4},{12,8},{16,12},{20,16},{24,20},{28,24},{5,1},{9,5},{13... | collective-permute-start | bytes 393224 | tf_op jit(solution)/shard_map/ppermute | solution.py:15
  135.8 15.7 %copy-start.4 = (bf16[128,16,64]{2,1,0:T(8,128)(2,1)}, bf16[128,16,64]{2,1,0:T(8,128)(2,1)S(1)}, u32[]{:S(2)}) copy-start(bf16[128,16,64]{2,1,0:T(8,128)(2,1)S(1)} %get-tuple-element.11) | copy-start | bytes 786436
  137.3 66.5 %all-gather.11.cloned.1.call-start = ((), (), s32[]{:S(2)}) async-start(), calls=%async_computation.3 | async-start | bytes 1310720 | tf_op jit(solution)/shard_map/all_gather | solution.py:46
  140.9 6.5 %collective-permute-start.4 = (bf16[64,1024]{1,0:T(8,128)(2,1)S(1)}, bf16[64,1024]{1,0:T(8,128)(2,1)S(1)}, u32[]{:S(2)}, u32[]{:S(2)}) collective-permute-start(bf16[64,1024]{1,0:T(8,128)(2,1)S(1)} %gather_fusion.6), channel_id=1, source_target_pairs={{0,4},{4,8},{8,12},{12,16},{16,20},{20,24},{24,28},{1,5},{5,9},{9,... | collective-permute-start | bytes 393224 | tf_op jit(solution)/shard_map/ppermute | solution.py:15
  144.3 7.2 %collective-permute-start.5 = (bf16[64,1024]{1,0:T(8,128)(2,1)S(1)}, bf16[64,1024]{1,0:T(8,128)(2,1)S(1)}, u32[]{:S(2)}, u32[]{:S(2)}) collective-permute-start(bf16[64,1024]{1,0:T(8,128)(2,1)S(1)} %gather_fusion.7), channel_id=1, source_target_pairs={{4,0},{8,4},{12,8},{16,12},{20,16},{24,20},{28,24},{5,1},{9,5},{13... | collective-permute-start | bytes 393224 | tf_op jit(solution)/shard_map/ppermute | solution.py:15
  185.4 15.7 %copy-start.6 = (bf16[128,16,64]{2,1,0:T(8,128)(2,1)}, bf16[128,16,64]{2,1,0:T(8,128)(2,1)S(1)}, u32[]{:S(2)}) copy-start(bf16[128,16,64]{2,1,0:T(8,128)(2,1)S(1)} %get-tuple-element.13) | copy-start | bytes 786436
  190.4 6.5 %collective-permute-start.6 = (bf16[64,1024]{1,0:T(8,128)(2,1)S(1)}, bf16[64,1024]{1,0:T(8,128)(2,1)S(1)}, u32[]{:S(2)}, u32[]{:S(2)}) collective-permute-start(bf16[64,1024]{1,0:T(8,128)(2,1)S(1)} %gather_fusion.9), channel_id=1, source_target_pairs={{0,4},{4,8},{8,12},{12,16},{16,20},{20,24},{24,28},{1,5},{5,9},{9,... | collective-permute-start | bytes 393224 | tf_op jit(solution)/shard_map/ppermute | solution.py:15
  193.8 7.2 %collective-permute-start.7 = (bf16[64,1024]{1,0:T(8,128)(2,1)S(1)}, bf16[64,1024]{1,0:T(8,128)(2,1)S(1)}, u32[]{:S(2)}, u32[]{:S(2)}) collective-permute-start(bf16[64,1024]{1,0:T(8,128)(2,1)S(1)} %gather_fusion.10), channel_id=1, source_target_pairs={{4,0},{8,4},{12,8},{16,12},{20,16},{24,20},{28,24},{5,1},{9,5},{13... | collective-permute-start | bytes 393224 | tf_op jit(solution)/shard_map/ppermute | solution.py:15
  234.9 4.7 %copy-start.1 = (bf16[128,5,64,16]{2,3,0,1:T(8,128)(2,1)S(1)}, bf16[128,5,64,16]{2,3,0,1:T(8,128)(2,1)}, u32[]{:S(2)}) copy-start(bf16[128,5,64,16]{2,3,0,1:T(8,128)(2,1)} %fusion.18) | copy-start | bytes 3932164
  314.7 2.8 copy-start.3
  314.8 2.8 copy-start.5
  314.8 2.8 copy-start.7
  315.3 2.2 copy-start.9
Sparse Core Ops, SparseCore 0:
  9.6 19.4 all-gather.4
  85.6 18.9 all-gather.6
  137.4 16.7 all-gather.8
  187.0 16.7 all-gather.10
